TPU v7x, 512 devices: a whole 4x8x8 slice. The times are simulated.
512 devices in a mesh: grp: 32 (over y, z_hi, core), leaf: 16 (over z_lo, x).
Axes of the slice: x: 4, y: 8, z: 8 (z_hi: 2, z_lo: 4; z = z_hi * 4 + z_lo), core: 2. Of those that a mesh axis runs over, the one named last changes fastest.
Arguments:
- vectors: bfloat16 [32, 2097152], P(None, ('grp', 'leaf')), may hold values from -6 to 6
- offsets: bfloat16 [3, 2097152], P(None, ('grp', 'leaf')), may hold values from 0 to 1
- near_list: int32 [8192, 16], P(('grp', 'leaf')), may hold values from 0 to 8191, as said below
- near_count: int32 [8192], P(('grp', 'leaf')), may hold values from 8 to 16, as said below
- leaf_basis: bfloat16 [8192, 64, 256], P(('grp', 'leaf')), may hold values from -0.375 to 0.375
- far_list: int32 [8192, 16], P(('grp', 'leaf')), may hold values from 0 to 8191, as said below
- far_count: int32 [8192], P(('grp', 'leaf')), may hold values from 0 to 16, as said below
- leaf_coupling: bfloat16 [8192, 16, 64, 64], P(('grp', 'leaf')), as said below
- transfer: bfloat16 [8192, 64, 64], P(('grp', 'leaf')), may hold values from -0.75 to 0.75
- group_list: int32 [32, 16], P('grp'), may hold values from 0 to 31, as said below
- group_count: int32 [32], P('grp'), may hold values from 8 to 16, as said below
- group_coupling: bfloat16 [32, 16, 64, 64], P('grp', 'leaf'), may hold values from -0.01171875 to 0.01171875
Outputs:
- applied: bfloat16 [32, 2097152], P(None, ('grp', 'leaf'))
Inputs may be any that keep to these rules, and one draw needn't show every extreme that they name: `near_list`: the first near_count[l] entries of row l are distinct leaves of l's own group lying on l's device or on the devices just before and after it along leaf (16 consecutive leaves a device); the first entry is l itself and the remaining entries repeat l. `near_count`: the first leaf of every device has exactly 16. `far_list`: the first far_count[l] entries of row l are distinct leaves of l's own group other than l; the remaining entries repeat l. If leaf j stands in slot k < far_count[l] of row l, then l stands in some slot k2 < far_count[j] of row j. `far_count`: the first leaf of every group has exactly 16. If far_list[l, k] = j with k < far_count[l], and far_list[j, k2] = l with k2 < far_count[j], then leaf_coupling[j, k2] is the transpose of leaf_coupling[l, k]. `group_list`: the first group_count[g] entries of row g are distinct groups other than g; the remaining entries repeat g. `group_count`: group 0 has exactly 16.
All inputs are finite; a program needn't handle non-finite values.
Results may differ from a plain program's by a relative error of at most 0.005.
Values may be sent and summed in bfloat16 or wider, within the bound.
No kernel may reach another device: no remote copies, remote signals or barrier semaphores. Data moves between devices by JAX's collectives and lax.ppermute only.
A program may use at most 64 MiB of HBM per device.

v0:
```python
import jax
import jax.numpy as jnp
from jax import lax
from jax.sharding import PartitionSpec as P

inv_four_pi = 0.07957747154594767
soften = 0.01


def with_halo(shard, sides, width):
    for axis, dim in sides:
        count, length = (lax.axis_size(axis), shard.shape[dim])
        up = [(i, (i + 1) % count) for i in range(count - 1)]
        down = [(j, i) for i, j in up]
        last = lax.slice_in_dim(shard, length - width, length, axis=dim)
        first = lax.slice_in_dim(shard, 0, width, axis=dim)
        before = lax.ppermute(last, axis, up)
        after = lax.ppermute(first, axis, down)
        shard = jnp.concatenate([before, shard, after], axis=dim)
    return shard


def centres(leaf_ids):
    columns = []
    for axis_pos in range(3):
        summed = jnp.zeros_like(leaf_ids)
        for bit_pos in range(10):
            picked = jnp.bitwise_and(jnp.right_shift(leaf_ids, 3 * bit_pos + axis_pos), 1)
            summed = summed + jnp.left_shift(picked, bit_pos)
        columns.append(summed.astype(jnp.float32))
    return jnp.stack(columns)


def kernel_tile(source_pts, target_pts):
    squared = jnp.zeros(
        (source_pts.shape[0], source_pts.shape[2], target_pts.shape[1]), jnp.float32
    )
    for axis_pos in range(3):
        spacing = source_pts[:, axis_pos, :, None] - target_pts[axis_pos][None, None, :]
        squared = squared + spacing * spacing
    return inv_four_pi * lax.rsqrt(squared + soften)


def body(
    vectors,
    offsets,
    near_list,
    near_count,
    leaf_basis,
    far_list,
    far_count,
    leaf_coupling,
    transfer,
    group_list,
    group_count,
    group_coupling,
):
    leaf_devices = lax.axis_size("leaf")
    local_leaves = near_list.shape[0]
    near_slots = near_list.shape[1]
    far_slots = far_list.shape[1]
    vec_count = vectors.shape[0]
    leaf_width = vectors.shape[1] // local_leaves
    group_leaves = leaf_devices * local_leaves
    leaf_place = lax.axis_index("leaf")
    group_place = lax.axis_index("grp")
    device_first = (group_place * leaf_devices + leaf_place) * local_leaves
    group_first = group_place * group_leaves
    window_first = device_first - local_leaves
    stacked = jnp.concatenate([vectors, offsets], axis=0)
    widened = with_halo(stacked, (("leaf", 1),), local_leaves * leaf_width)
    window_vectors = widened[:vec_count].reshape(vec_count, 3 * local_leaves, leaf_width)
    window_ids = window_first + jnp.arange(3 * local_leaves, dtype=jnp.int32)
    window_pts = (
        widened[vec_count:].astype(jnp.float32).reshape(3, 3 * local_leaves, leaf_width)
        + centres(window_ids)[:, :, None]
    )
    slot_ids = jnp.arange(near_slots, dtype=jnp.int32)

    def near_step(running, target):
        sources = near_list[target] - window_first
        active_slots = slot_ids < near_count[target]
        source_pts = jnp.take(window_pts, sources, axis=1).transpose(1, 0, 2)
        target_pts = lax.dynamic_index_in_dim(window_pts, local_leaves + target, 1, keepdims=False)
        near_tile = jnp.where(
            active_slots[:, None, None], kernel_tile(source_pts, target_pts), 0.0
        ).astype(jnp.bfloat16)
        source_vectors = jnp.take(window_vectors, sources, axis=1)
        return (
            running,
            jnp.einsum(
                "vkb,kba->va", source_vectors, near_tile, preferred_element_type=jnp.float32
            ),
        )

    ignored, near_field = lax.scan(near_step, 0, jnp.arange(local_leaves, dtype=jnp.int32))
    leaf_vectors = vectors.reshape(vec_count, local_leaves, leaf_width)
    coeffs = jnp.einsum(
        "via,ira->ivr", leaf_vectors, leaf_basis, preferred_element_type=jnp.float32
    ).astype(jnp.bfloat16)
    far_active = jnp.arange(far_slots, dtype=jnp.int32)[None, :] < far_count[:, None]
    far_rows = far_list - group_first
    group_coeffs = lax.all_gather(coeffs, "leaf", axis=0, tiled=True)
    picked = jnp.take(group_coeffs, far_rows, axis=0)
    picked = jnp.where(far_active[:, :, None, None], picked, jnp.zeros((), jnp.bfloat16))
    far_field = jnp.einsum(
        "ikvs,ikrs->ivr", picked, leaf_coupling, preferred_element_type=jnp.float32
    )
    coarse_part = jnp.einsum("ivs,isr->vr", coeffs, transfer, preferred_element_type=jnp.float32)
    coarse = lax.psum(coarse_part, "leaf").astype(jnp.bfloat16)
    all_coarse = lax.all_gather(coarse[None], "grp", axis=0, tiled=True)
    group_active = jnp.arange(group_list.shape[1], dtype=jnp.int32) < group_count[0]
    own_slots = group_coupling.shape[1]
    slot_first = leaf_place * own_slots
    own_groups = lax.dynamic_slice_in_dim(group_list[0], slot_first, own_slots, 0)
    own_active = lax.dynamic_slice_in_dim(group_active, slot_first, own_slots, 0)
    picked_groups = jnp.where(
        own_active[:, None, None],
        jnp.take(all_coarse, own_groups, axis=0),
        jnp.zeros((), jnp.bfloat16),
    )
    coarse_term = jnp.einsum(
        "kvs,krs->vr", picked_groups, group_coupling[0], preferred_element_type=jnp.float32
    )
    coarse_out = lax.psum(coarse_term, "leaf")
    downward = jnp.einsum(
        "vs,irs->ivr", coarse_out.astype(jnp.bfloat16), transfer, preferred_element_type=jnp.float32
    )
    local_coeffs = (far_field + downward).astype(jnp.bfloat16)
    expanded = jnp.einsum(
        "ivr,ira->via", local_coeffs, leaf_basis, preferred_element_type=jnp.float32
    )
    result = jnp.transpose(near_field, (1, 0, 2)) + expanded
    return result.reshape(vec_count, local_leaves * leaf_width).astype(jnp.bfloat16)


def solution(mesh):
    placed = (
        P(None, ("grp", "leaf")),
        P(None, ("grp", "leaf")),
        P(("grp", "leaf"), None),
        P(("grp", "leaf")),
        P(("grp", "leaf"), None, None),
        P(("grp", "leaf"), None),
        P(("grp", "leaf")),
        P(("grp", "leaf"), None, None, None),
        P(("grp", "leaf"), None, None),
        P("grp", None),
        P("grp"),
        P("grp", "leaf", None, None),
    )
    return jax.shard_map(
        body, mesh=mesh, in_specs=placed, out_specs=P(None, ("grp", "leaf")), check_vma=False
    )
```

profile of v0, /device:TPU:8, one launch (start us, length us, event | category | flops | bytes accessed | tf_op | source)
XLA Modules:
  0.0 398.0 jit_solution(17522042291182980777)
XLA Ops:
  6.5 1.0 constant_dynamic-update-slice_fusion.1
  7.6 0.8 constant_dynamic-update-slice_fusion
  8.4 1.3 collective-permute-start.1
  9.7 4.6 %collective-permute-start = (bf16[35,4096]{1,0:T(8,128)(2,1)S(1)}, bf16[35,4096]{1,0:T(8,128)(2,1)S(1)}, u32[]{:S(2)}, u32[]{:S(2)}) collective-permute-start(bf16[35,4096]{1,0:T(8,128)(2,1)S(1)} %constant_dynamic-update-slice_fusion), channel_id=1, source_target_pairs={{0,1},{1,2},{2,3},{3,4},{4,5},{5,6},{6,7},{7,8},{8,9},{9,10},{10,1... | collective-permute-start | bytes 860168 | tf_op jit(solution)/shard_map/ppermute | solution.py:17
  14.3 1.9 convolution_convert_fusion
  17.5 1.2 constant_dynamic-slice_fusion.4
  21.3 1.2 convolution_bitcast_fusion.1
  22.5 80.5 %psum.14 = bf16[32,64]{1,0:T(8,128)(2,1)S(1)} all-reduce(f32[32,64]{1,0:T(8,128)S(1)} %convolution_bitcast_fusion.1), channel_id=1, replica_groups=mesh['grp'=32,'leaf'=16] {'leaf'}, use_global_device_ids=true, to_apply=%region_2.3 | all-reduce | flops 2048 | bytes 12288 | tf_op jit(solution)/shard_map/psum | solution.py:110
  103.0 53.7 %all-gather = bf16[1024,64]{1,0:T(8,128)(2,1)S(1)} all-gather(bf16[32,64]{1,0:T(8,128)(2,1)S(1)} %psum.14), channel_id=2, replica_groups=mesh['grp'=32,'leaf'=16] {'grp'}, dimensions={0}, use_global_device_ids=true | all-gather | bytes 135168 | tf_op jit(solution)/shard_map/all_gather | solution.py:111
  156.7 1.5 fusion.30
  158.2 74.2 %psum.15 = bf16[32,64]{1,0:T(8,128)(2,1)S(1)} all-reduce(f32[32,64]{1,0:T(8,128)S(1)} %fusion.30), channel_id=1, replica_groups=mesh['grp'=32,'leaf'=16] {'leaf'}, use_global_device_ids=true, to_apply=%region_3.4 | all-reduce | flops 2048 | bytes 12288 | tf_op jit(solution)/shard_map/psum | solution.py:125
  232.5 0.7 iota_compare_fusion
  233.6 148.9 %while.15 = (s32[]{:T(128)}, f32[16,32,256]{2,1,0:T(8,128)S(1)}, s32[16]{0:T(128)S(1)}, s32[16,16]{1,0:T(8,128)}, s32[]{:T(128)}, /*index=5*/bf16[32,48,256]{2,0...) while((s32[]{:T(128)}, f32[16,32,256]{2,1,0:T(8,128)S(1)}, ...), condition=%wide.region_1.2_spmd.clone, body=%wide.region_0.1_spmd.clone.sunk | while | flops 79836360 | bytes 1276693 | solution.py:96
  238.3 1.4 compare_and_fusion.3
  241.1 1.9 fusion.62
  247.7 1.4 compare_and_fusion.3
  250.4 1.9 fusion.62
  257.0 1.4 compare_and_fusion.3
  259.7 1.9 fusion.62
  266.3 1.4 compare_and_fusion.3
  269.0 1.9 fusion.62
  275.6 1.4 compare_and_fusion.3
  278.3 1.9 fusion.62
  284.9 1.4 compare_and_fusion.3
  287.6 1.9 fusion.62
  294.2 1.4 compare_and_fusion.3
  296.9 1.9 fusion.62
  303.5 1.4 compare_and_fusion.3
  306.2 1.9 fusion.62
  312.8 1.4 compare_and_fusion.3
  315.6 1.9 fusion.62
  322.1 1.4 compare_and_fusion.3
  324.9 1.9 fusion.62
  331.4 1.4 compare_and_fusion.3
  334.2 1.9 fusion.62
  340.7 1.4 compare_and_fusion.3
  343.5 1.9 fusion.62
  350.0 1.4 compare_and_fusion.3
  352.8 1.9 fusion.62
  359.3 1.4 compare_and_fusion.3
  362.1 1.9 fusion.62
  368.7 1.4 compare_and_fusion.3
  371.4 1.9 fusion.62
  378.0 1.4 compare_and_fusion.3
  380.7 1.9 fusion.62
  382.6 2.6 gather_fusion.2
  385.2 3.8 fusion.20
  389.0 1.4 fusion.23
  (220 shorter events, 55.7 us)
Async XLA Ops:
  6.5 7.7 %copy-start = (bf16[16,64,256]{2,1,0:T(8,128)(2,1)S(1)}, bf16[16,64,256]{2,1,0:T(8,128)(2,1)}, u32[]{:S(2)}) copy-start(bf16[16,64,256]{2,1,0:T(8,128)(2,1)} %param.18) | copy-start | bytes 1572868
  6.5 376.0 %all-gather.3.cloned.1.call-start = ((), (), s32[]{:S(2)}) async-start(), calls=%async_computation | async-start | bytes 2228224 | tf_op jit(solution)/shard_map/all_gather | solution.py:103
  8.4 224.9 %collective-permute-start.1 = (bf16[35,4096]{1,0:T(8,128)(2,1)S(1)}, bf16[35,4096]{1,0:T(8,128)(2,1)S(1)}, u32[]{:S(2)}, u32[]{:S(2)}) collective-permute-start(bf16[35,4096]{1,0:T(8,128)(2,1)S(1)} %constant_dynamic-update-slice_fusion), channel_id=1, source_target_pairs={{1,0},{2,1},{3,2},{4,3},{5,4},{6,5},{7,6},{8,7},{9,8},{10,9},{11,1... | collective-permute-start | bytes 860168 | tf_op jit(solution)/shard_map/ppermute | solution.py:18
  9.7 223.6 %collective-permute-start = (bf16[35,4096]{1,0:T(8,128)(2,1)S(1)}, bf16[35,4096]{1,0:T(8,128)(2,1)S(1)}, u32[]{:S(2)}, u32[]{:S(2)}) collective-permute-start(bf16[35,4096]{1,0:T(8,128)(2,1)S(1)} %constant_dynamic-update-slice_fusion), channel_id=1, source_target_pairs={{0,1},{1,2},{2,3},{3,4},{4,5},{5,6},{6,7},{7,8},{8,9},{9,10},{10,1... | collective-permute-start | bytes 860168 | tf_op jit(solution)/shard_map/ppermute | solution.py:17
  14.2 219.4 %copy-start.2 = (s32[16]{0:T(128)S(1)}, s32[16]{0:T(128)}, u32[]{:S(2)}) copy-start(s32[16]{0:T(128)} %param.17) | copy-start | bytes 196
  385.2 3.8 copy-start.1
Sparse Core Ops, SparseCore 0:
  16.3 92.5 all-gather.2
where the time goes:
time: 400 us; the launch traced here: 398 us
  blocking collectives  208 us (52%)
  local copies, waits for them, and re-layouts  47.7 us (12%)
  loops' own time  44.3 us (11%)
  matrix products  39.6 us (10%)
  other arithmetic  36.2 us (9%)
  between operations  15.9 us (4%)
  starting transfers between devices  5.86 us (1%)
    psum x1, blocking collectives, body(): coarse = lax.psum(coarse_part, 'leaf').astype(jnp.bfloat16)  80.5 us
    psum x1, blocking collectives, body(): coarse_out = lax.psum(coarse_term, 'leaf')  74.2 us
    all_gather x1, blocking collectives, body(): all_coarse = lax.all_gather(coarse[None], 'grp', axis=0, tiled=True)  53.7 us
    another operation x1, loops' own time, body(): lax.scan(near_step, 0, jnp.arange(local_leaves, dtype=jnp.int32))  44.3 us
    dot_general x16, matrix products, near_step(): jnp.einsum('vkb,kba->va', source_vectors, near_tile, preferred_element_ty...  29.8 us
    and x16, other arithmetic, near_step(): source_vectors = jnp.take(window_vectors, sources, axis=1)  21.9 us
    select_n x16, other arithmetic, near_step(): source_vectors = jnp.take(window_vectors, sources, axis=1)  11.1 us
    dynamic_slice x16, local copies, waits for them, and re-layouts, body(): lax.scan(near_step, 0, jnp.arange(local_leaves, dtype=jnp.int32))  10.5 us
  transfers between devices with their start and end apart: 3, of which 0 were waited for; matrix products, arithmetic and copies ran while one was open for 28% of the time, Pallas kernels for 0%

commit v1 on v0

--- a/solution.py
+++ b/solution.py
@@ -108,7 +108,11 @@
     )
     coarse_part = jnp.einsum("ivs,isr->vr", coeffs, transfer, preferred_element_type=jnp.float32)
     coarse = lax.psum(coarse_part, "leaf").astype(jnp.bfloat16)
-    all_coarse = lax.all_gather(coarse[None], "grp", axis=0, tiled=True)
+    x = coarse[None]
+    size = lax.axis_size("grp")
+    blocks = jnp.stack([x for _ in range(size)])
+    blocks = lax.all_to_all(blocks, "grp", split_axis=0, concat_axis=0)
+    all_coarse = jnp.concatenate(blocks, axis=0)
     group_active = jnp.arange(group_list.shape[1], dtype=jnp.int32) < group_count[0]
     own_slots = group_coupling.shape[1]
     slot_first = leaf_place * own_slots

time: 400 us -> 368 us (0.920)
  blocking collectives: 208 us -> 155 us
  starting transfers between devices: 5.86 us -> 19.3 us
  waiting for transfers between devices: 0.03 us -> 6.85 us
    all_gather x1 -> x0, blocking collectives: 53.7 us -> none  [body(): all_coarse = lax.all_gather(coarse[None], 'grp', axis=0, tiled=True)]
    all_to_all x0 -> x1, starting transfers between devices: none -> 13.5 us  [body(): blocks = lax.all_to_all(blocks, 'grp', split_axis=0, concat_axis=0)]
    all_to_all x0 -> x1, waiting for transfers between devices: none -> 6.83 us  [body(): blocks = lax.all_to_all(blocks, 'grp', split_axis=0, concat_axis=0)]
  transfers between devices with their start and end apart: 3 -> 4, of which waited for: 0 -> 1; matrix products, arithmetic and copies ran while one was open for 28% -> 31% of each run, Pallas kernels for 0% -> 0%
where the time goes in v1:
time: 368 us; the launch traced here: 366 us
  blocking collectives  155 us (42%)
  local copies, waits for them, and re-layouts  48.7 us (13%)
  loops' own time  44.3 us (12%)
  matrix products  39.6 us (11%)
  other arithmetic  36.2 us (10%)
  starting transfers between devices  19.3 us (5%)
  between operations  16.1 us (4%)
  waiting for transfers between devices  6.85 us (2%)
    psum x1, blocking collectives, body(): coarse = lax.psum(coarse_part, 'leaf').astype(jnp.bfloat16)  80.5 us
    psum x1, blocking collectives, body(): coarse_out = lax.psum(coarse_term, 'leaf')  74.3 us
    another operation x1, loops' own time, body(): lax.scan(near_step, 0, jnp.arange(local_leaves, dtype=jnp.int32))  44.3 us
    dot_general x16, matrix products, near_step(): jnp.einsum('vkb,kba->va', source_vectors, near_tile, preferred_element_ty...  29.8 us
    and x16, other arithmetic, near_step(): source_vectors = jnp.take(window_vectors, sources, axis=1)  21.9 us
    all_to_all x1, starting transfers between devices, body(): blocks = lax.all_to_all(blocks, 'grp', split_axis=0, concat_axis=0)  13.5 us
    select_n x16, other arithmetic, near_step(): source_vectors = jnp.take(window_vectors, sources, axis=1)  11.1 us
    dynamic_slice x16, local copies, waits for them, and re-layouts, body(): lax.scan(near_step, 0, jnp.arange(local_leaves, dtype=jnp.int32))  10.5 us
  transfers between devices with their start and end apart: 4, of which 1 were waited for; matrix products, arithmetic and copies ran while one was open for 31% of the time, Pallas kernels for 0%

profile of v1, /device:TPU:8, one launch (start us, length us, event | category | flops | bytes accessed | tf_op | source)
XLA Modules:
  0.0 365.8 jit_solution(73190281715758642)
XLA Ops:
  6.5 1.0 constant_dynamic-update-slice_fusion.1
  8.4 1.3 collective-permute-start.1
  9.7 4.6 %collective-permute-start = (bf16[35,4096]{1,0:T(8,128)(2,1)S(1)}, bf16[35,4096]{1,0:T(8,128)(2,1)S(1)}, u32[]{:S(2)}, u32[]{:S(2)}) collective-permute-start(bf16[35,4096]{1,0:T(8,128)(2,1)S(1)} %constant_dynamic-update-slice_fusion), channel_id=1, source_target_pairs={{0,1},{1,2},{2,3},{3,4},{4,5},{5,6},{6,7},{7,8},{8,9},{9,10},{10,1... | collective-permute-start | bytes 860168 | tf_op jit(solution)/shard_map/ppermute | solution.py:17
  14.2 1.9 convolution_convert_fusion
  16.2 1.2 convolution_bitcast_fusion.1
  17.4 80.5 %psum.14 = bf16[32,64]{1,0:T(8,128)(2,1)S(1)} all-reduce(f32[32,64]{1,0:T(8,128)S(1)} %convolution_bitcast_fusion.1), channel_id=1, replica_groups=mesh['grp'=32,'leaf'=16] {'leaf'}, use_global_device_ids=true, to_apply=%region_2.3 | all-reduce | flops 2048 | bytes 12288 | tf_op jit(solution)/shard_map/psum | solution.py:110
  98.0 0.8 reshape.569
  98.8 13.5 %all-to-all-start = ((bf16[32,2,1024]{2,1,0:T(2,128)(2,1)}), bf16[32,2,1024]{2,1,0:T(2,128)(2,1)S(1)}, u32[]{:S(2)}, u32[]{:S(2)}) async-start(bf16[32,2,1024]{2,1,0:T(2,128)(2,1)} %reshape.569), calls=%async_computation | async-start | bytes 262144 | tf_op jit(solution)/shard_map/all_to_all | solution.py:114
  115.2 1.2 constant_dynamic-slice_fusion.4
  118.4 6.8 %all-to-all-done = bf16[32,2,1024]{2,1,0:T(2,128)(2,1)S(1)} async-done(((bf16[32,2,1024]{2,1,0:T(2,128)(2,1)}), bf16[32,2,1024]{2,1,0:T(2,128)(2,1)S(1)}, u32[]{:S(2)}, u32[]{:S(2)}) %all-to-all-start) | async-done | bytes 131104 | tf_op jit(solution)/shard_map/all_to_all | solution.py:114
  125.4 1.4 fusion.30
  126.8 74.3 %psum.15 = bf16[32,64]{1,0:T(8,128)(2,1)S(1)} all-reduce(f32[32,64]{1,0:T(8,128)S(1)} %fusion.30), channel_id=1, replica_groups=mesh['grp'=32,'leaf'=16] {'leaf'}, use_global_device_ids=true, to_apply=%region_3.4 | all-reduce | flops 2048 | bytes 12288 | tf_op jit(solution)/shard_map/psum | solution.py:129
  201.5 148.8 %while.15 = (s32[]{:T(128)}, f32[16,32,256]{2,1,0:T(8,128)S(1)}, s32[16]{0:T(128)S(1)}, s32[16,16]{1,0:T(8,128)}, s32[]{:T(128)}, /*index=5*/bf16[32,48,256]{2,0...) while((s32[]{:T(128)}, f32[16,32,256]{2,1,0:T(8,128)S(1)}, ...), condition=%wide.region_1.2_spmd.clone, body=%wide.region_0.1_spmd.clone.sunk | while | flops 79836360 | bytes 1276693 | solution.py:96
  206.2 1.4 compare_and_fusion.3
  209.0 1.9 fusion.63
  215.5 1.4 compare_and_fusion.3
  218.3 1.9 fusion.63
  224.8 1.4 compare_and_fusion.3
  227.6 1.9 fusion.63
  234.2 1.4 compare_and_fusion.3
  236.9 1.9 fusion.63
  243.5 1.4 compare_and_fusion.3
  246.2 1.9 fusion.63
  252.8 1.4 compare_and_fusion.3
  255.5 1.9 fusion.63
  262.1 1.4 compare_and_fusion.3
  264.8 1.9 fusion.63
  271.4 1.4 compare_and_fusion.3
  274.1 1.9 fusion.63
  280.7 1.4 compare_and_fusion.3
  283.4 1.9 fusion.63
  290.0 1.4 compare_and_fusion.3
  292.7 1.9 fusion.63
  299.3 1.4 compare_and_fusion.3
  302.0 1.9 fusion.63
  308.6 1.4 compare_and_fusion.3
  311.3 1.9 fusion.63
  317.9 1.4 compare_and_fusion.3
  320.6 1.9 fusion.63
  327.2 1.4 compare_and_fusion.3
  329.9 1.9 fusion.63
  336.5 1.4 compare_and_fusion.3
  339.2 1.9 fusion.63
  345.8 1.4 compare_and_fusion.3
  348.5 1.9 fusion.63
  350.4 2.6 gather_fusion.2
  353.0 3.8 %fusion.20 = f32[16,32,64]{2,1,0:T(8,128)} fusion(bf16[16,16,64,64]{3,2,1,0:T(8,128)(2,1)} %param.21, bf16[16,16,32,64]{3,2,1,0:T(8,128)(2,1)S(1)} %bitcast.106, pred[16,16]{1,0:T(8,128)(4,1)S(1)} %get-tuple-element.195, pred[16,16]{1,0:T(8,128)(4,1)S(1)} %iota_compare_fusion), kind=kOutput, calls=%fused_computation.38 | convolution fusion | flops 68157440 | bytes 3277312 | tf_op jit(solution)/shard_map/ikvs,ikrs->ivr/dot_general | solution.py:106
  356.8 1.4 fusion.23
  (224 shorter events, 57.3 us)
Async XLA Ops:
  6.5 7.7 %copy-start = (bf16[16,64,256]{2,1,0:T(8,128)(2,1)S(1)}, bf16[16,64,256]{2,1,0:T(8,128)(2,1)}, u32[]{:S(2)}) copy-start(bf16[16,64,256]{2,1,0:T(8,128)(2,1)} %param.18) | copy-start | bytes 1572868
  6.5 343.8 %all-gather.2.cloned.1.call-start = ((), (), s32[]{:S(2)}) async-start(), calls=%async_computation.1 | async-start | bytes 2228224 | tf_op jit(solution)/shard_map/all_gather | solution.py:103
  8.4 192.8 %collective-permute-start.1 = (bf16[35,4096]{1,0:T(8,128)(2,1)S(1)}, bf16[35,4096]{1,0:T(8,128)(2,1)S(1)}, u32[]{:S(2)}, u32[]{:S(2)}) collective-permute-start(bf16[35,4096]{1,0:T(8,128)(2,1)S(1)} %constant_dynamic-update-slice_fusion), channel_id=1, source_target_pairs={{1,0},{2,1},{3,2},{4,3},{5,4},{6,5},{7,6},{8,7},{9,8},{10,9},{11,1... | collective-permute-start | bytes 860168 | tf_op jit(solution)/shard_map/ppermute | solution.py:18
  9.7 191.5 %collective-permute-start = (bf16[35,4096]{1,0:T(8,128)(2,1)S(1)}, bf16[35,4096]{1,0:T(8,128)(2,1)S(1)}, u32[]{:S(2)}, u32[]{:S(2)}) collective-permute-start(bf16[35,4096]{1,0:T(8,128)(2,1)S(1)} %constant_dynamic-update-slice_fusion), channel_id=1, source_target_pairs={{0,1},{1,2},{2,3},{3,4},{4,5},{5,6},{6,7},{7,8},{8,9},{9,10},{10,1... | collective-permute-start | bytes 860168 | tf_op jit(solution)/shard_map/ppermute | solution.py:17
  16.1 185.4 %copy-start.2 = (s32[16]{0:T(128)S(1)}, s32[16]{0:T(128)}, u32[]{:S(2)}) copy-start(s32[16]{0:T(128)} %param.17) | copy-start | bytes 196
  98.8 26.4 %all-to-all-start = ((bf16[32,2,1024]{2,1,0:T(2,128)(2,1)}), bf16[32,2,1024]{2,1,0:T(2,128)(2,1)S(1)}, u32[]{:S(2)}, u32[]{:S(2)}) async-start(bf16[32,2,1024]{2,1,0:T(2,128)(2,1)} %reshape.569), calls=%async_computation | async-start | bytes 262144 | tf_op jit(solution)/shard_map/all_to_all | solution.py:114
  353.0 3.8 %copy-start.1 = (bf16[16,64,64]{2,1,0:T(8,128)(2,1)S(1)}, bf16[16,64,64]{2,1,0:T(8,128)(2,1)}, u32[]{:S(2)}) copy-start(bf16[16,64,64]{2,1,0:T(8,128)(2,1)} %param.22) | copy-start | bytes 393220
Sparse Core Ops, SparseCore 0:
  16.3 92.3 all-gather.1
